TPU v7x, 32 devices: a whole 2x2x4 slice. The times are simulated.
32 devices in a mesh: dp: 2 (over core), ctx: 8 (over z, y), fsdp: 2 (over x).
Axes of the slice: x: 2, y: 2, z: 4, core: 2. Of those that a mesh axis runs over, the one named last changes fastest.
Arguments:
- tokens: bfloat16 [4, 1024, 1152], P(('dp', 'fsdp'), 'ctx'), may hold values from -6 to 6
- cotangent: bfloat16 [4, 1024, 1152], P(('dp', 'fsdp'), 'ctx'), may hold values from -6 to 6
- segments: int32 [4, 1024], P(('dp', 'fsdp')), may hold values from 0 to 15, never falling along the last dimension, each value on 1 to 640 neighbouring positions
- qkv_weight: float32 [1536, 1152], P(('ctx', 'fsdp')), may hold values from -0.1875 to 0.1875
- out_weight: float32 [1024, 1152], P(('ctx', 'fsdp')), may hold values from -0.1875 to 0.1875
- gate_up_weight: float32 [13824, 1152], P(('ctx', 'fsdp')), may hold values from -0.1875 to 0.1875
- down_weight: float32 [6912, 1152], P(('ctx', 'fsdp')), may hold values from -0.078125 to 0.078125
- gains: float32 [5120], P(('ctx', 'fsdp')), may hold values from -0.15 to 0.15
- qkv_first: float32 [1536, 1152], P(('ctx', 'fsdp')), may hold values from -90 to 90
- out_first: float32 [1024, 1152], P(('ctx', 'fsdp')), may hold values from -90 to 90
- gate_up_first: float32 [13824, 1152], P(('ctx', 'fsdp')), may hold values from -90 to 90
- down_first: float32 [6912, 1152], P(('ctx', 'fsdp')), may hold values from -90 to 90
- gains_first: float32 [5120], P(('ctx', 'fsdp')), may hold values from -90 to 90
- qkv_second: float32 [1536, 1152], P(('ctx', 'fsdp')), may hold values from 300 to 3000
- out_second: float32 [1024, 1152], P(('ctx', 'fsdp')), may hold values from 300 to 3000
- gate_up_second: float32 [13824, 1152], P(('ctx', 'fsdp')), may hold values from 300 to 3000
- down_second: float32 [6912, 1152], P(('ctx', 'fsdp')), may hold values from 300 to 3000
- gains_second: float32 [5120], P(('ctx', 'fsdp')), may hold values from 300 to 3000
Outputs:
- output: bfloat16 [4, 1024, 1152], P(('dp', 'fsdp'), 'ctx')
- input_grad: float32 [4, 1024, 1152], P(('dp', 'fsdp'), 'ctx')
- qkv_grad: float32 [1536, 1152], P(('ctx', 'fsdp'))
- out_grad: float32 [1024, 1152], P(('ctx', 'fsdp'))
- gate_up_grad: float32 [13824, 1152], P(('ctx', 'fsdp'))
- down_grad: float32 [6912, 1152], P(('ctx', 'fsdp'))
- gains_grad: float32 [5120], P(('ctx', 'fsdp'))
- qkv_new: float32 [1536, 1152], P(('ctx', 'fsdp'))
- out_new: float32 [1024, 1152], P(('ctx', 'fsdp'))
- gate_up_new: float32 [13824, 1152], P(('ctx', 'fsdp'))
- down_new: float32 [6912, 1152], P(('ctx', 'fsdp'))
- gains_new: float32 [5120], P(('ctx', 'fsdp'))
- qkv_first_new: float32 [1536, 1152], P(('ctx', 'fsdp'))
- out_first_new: float32 [1024, 1152], P(('ctx', 'fsdp'))
- gate_up_first_new: float32 [13824, 1152], P(('ctx', 'fsdp'))
- down_first_new: float32 [6912, 1152], P(('ctx', 'fsdp'))
- gains_first_new: float32 [5120], P(('ctx', 'fsdp'))
- qkv_second_new: float32 [1536, 1152], P(('ctx', 'fsdp'))
- out_second_new: float32 [1024, 1152], P(('ctx', 'fsdp'))
- gate_up_second_new: float32 [13824, 1152], P(('ctx', 'fsdp'))
- down_second_new: float32 [6912, 1152], P(('ctx', 'fsdp'))
- gains_second_new: float32 [5120], P(('ctx', 'fsdp'))
Inputs may be any that keep to these rules, and one draw needn't show every extreme that they name: `segments`: in each sequence the segment numbers never fall, every number appears, each document has 1 to 640 tokens, and one has exactly 640.
All inputs are finite; a program needn't handle non-finite values.
Results may differ from a plain program's by a relative error of at most 0.018.
Values may be sent and summed in bfloat16 or wider, within the bound.
A program may use at most 320 MiB of HBM per device.

v0:
```python
import jax
import jax.numpy as jnp
from jax import lax
from jax.sharding import PartitionSpec as P

H = 4
HD = 256
STEP = 5


def normalize(value, gain):
    scale = lax.rsqrt(jnp.mean(value * value, axis=-1, keepdims=True) + 1e-06)
    return value * scale * (1.0 + gain)


def rotate(value, angles):
    half = value.shape[-1] // 2
    first = value[..., :half]
    second = value[..., half:]
    cosine = jnp.cos(angles)
    sine = jnp.sin(angles)
    return jnp.concatenate(
        [first * cosine - second * sine, second * cosine + first * sine], axis=-1
    )


def rope_angles(segments):
    count = segments.shape[0]
    index = jnp.arange(count, dtype=jnp.int32)
    change = jnp.concatenate([jnp.ones((1,), dtype=jnp.bool_), segments[1:] != segments[:-1]])
    starts = lax.cummax(jnp.where(change, index, 0), axis=0)
    offset = (index - starts).astype(jnp.float32)
    inverse = jnp.exp(-jnp.log(1000000.0) * (2.0 * jnp.arange(HD // 2, dtype=jnp.float32)) / HD)
    return offset[:, None] * inverse[None, :]


def contract_last(left, right):
    return lax.dot_general(
        left, right, (((1,), (1,)), ((), ())), preferred_element_type=jnp.float32
    )


def contract_first(left, right):
    return lax.dot_general(
        left, right, (((0,), (0,)), ((), ())), preferred_element_type=jnp.float32
    )


def activate(gate_up):
    half = gate_up.shape[-1] // 2
    return jax.nn.gelu(gate_up[:, :half], approximate=True) * gate_up[:, half:]


def adamw(weight, grad, first, second):
    first_new = 0.9 * first + 0.1 * grad
    second_new = 0.95 * second + 0.05 * grad * grad
    first_hat = first_new / (1.0 - 0.9**STEP)
    second_hat = second_new / (1.0 - 0.95**STEP)
    weight_new = weight - 0.03 * (first_hat / (jnp.sqrt(second_hat) + 1e-08) + 0.1 * weight)
    return (weight_new, first_new, second_new)


def body(
    tokens,
    cotangent,
    segments,
    qkv_weight,
    out_weight,
    gate_up_weight,
    down_weight,
    gains,
    qkv_first,
    out_first,
    gate_up_first,
    down_first,
    gains_first,
    qkv_second,
    out_second,
    gate_up_second,
    down_second,
    gains_second,
):
    rows = tokens.shape[1]
    width = tokens.shape[2]
    length = segments.shape[1]
    query_width = H * HD
    scale = HD ** (-0.5)
    reach = lax.axis_size("ctx") // 2 + 1
    front = reach * rows
    window = front + rows
    qkv_full, out_full, gains_full = (
        lax.all_gather(qkv_weight.astype(jnp.bfloat16), ("ctx", "fsdp"), axis=0, tiled=True),
        lax.all_gather(out_weight.astype(jnp.bfloat16), ("ctx", "fsdp"), axis=0, tiled=True),
        lax.all_gather(gains.astype(jnp.bfloat16), ("ctx", "fsdp"), axis=0, tiled=True),
    )
    gain_all = gains_full.astype(jnp.float32)
    gain_input = gain_all[:width]
    gain_attend = gain_all[width : 2 * width]
    gain_pre = gain_all[2 * width : 3 * width]
    gain_post = gain_all[3 * width : 4 * width]
    gain_query = gain_all[4 * width : 4 * width + HD]
    gain_key = gain_all[4 * width + HD :]
    first_row = lax.axis_index("ctx") * rows
    sequence_ids = segments[0]
    angles = lax.dynamic_slice_in_dim(rope_angles(sequence_ids), first_row, rows, 0)
    query_ids = lax.dynamic_slice_in_dim(sequence_ids, first_row, rows, 0)
    query_pos = first_row + jnp.arange(rows, dtype=jnp.int32)
    window_pos = first_row - front + jnp.arange(window, dtype=jnp.int32)
    padded_ids = jnp.concatenate([jnp.full((front,), -1, dtype=jnp.int32), sequence_ids])
    window_ids = lax.dynamic_slice_in_dim(padded_ids, first_row, window, 0)
    allowed = (window_pos[None, :] <= query_pos[:, None]) & (
        window_ids[None, :] == query_ids[:, None]
    )
    allowed = allowed[:, None, :]
    x_rows = tokens[0].astype(jnp.float32)
    normed, input_back = jax.vjp(normalize, x_rows, gain_input)
    normed_low = normed.astype(jnp.bfloat16)
    projected = contract_last(normed_low, qkv_full)
    proj_query = projected[:, :query_width].reshape(rows, H, HD)
    proj_key = projected[:, query_width : query_width + HD]
    proj_value = projected[:, query_width + HD :]

    def query_key(part_query, part_key, query_gain, key_gain):
        return (
            rotate(normalize(part_query, query_gain), angles[:, None, :]),
            rotate(normalize(part_key, key_gain), angles),
        )

    (rotated_query, rotated_key), rotate_back = jax.vjp(
        query_key, proj_query, proj_key, gain_query, gain_key
    )
    query = rotated_query.astype(jnp.bfloat16)
    key_low = rotated_key.astype(jnp.bfloat16)
    value_low = proj_value.astype(jnp.bfloat16)
    keys_all, values_all = (
        lax.all_gather(key_low, "ctx", axis=0, tiled=True),
        lax.all_gather(value_low, "ctx", axis=0, tiled=True),
    )
    blank = jnp.zeros((front, HD), jnp.bfloat16)
    keys = lax.dynamic_slice_in_dim(jnp.concatenate([blank, keys_all]), first_row, window, 0)
    values = lax.dynamic_slice_in_dim(jnp.concatenate([blank, values_all]), first_row, window, 0)
    scores = jnp.einsum("thd,ld->thl", query, keys, preferred_element_type=jnp.float32) * scale
    masked = jnp.where(allowed, scores, -1e30)
    largest = jnp.max(masked, axis=-1, keepdims=True)
    log_total = largest + jnp.log(jnp.sum(jnp.exp(masked - largest), axis=-1, keepdims=True))
    probs_low = jnp.exp(masked - log_total).astype(jnp.bfloat16)
    attended = jnp.einsum("thl,ld->thd", probs_low, values, preferred_element_type=jnp.float32)
    attended = attended.reshape(rows, query_width).astype(jnp.bfloat16)
    branch = jnp.dot(attended, out_full, preferred_element_type=jnp.float32)
    branch_normed, attend_back = jax.vjp(normalize, branch, gain_attend)
    hidden = x_rows + branch_normed
    gate_up_full, down_full = (
        lax.all_gather(gate_up_weight.astype(jnp.bfloat16), ("ctx", "fsdp"), axis=0, tiled=True),
        lax.all_gather(down_weight.astype(jnp.bfloat16), ("ctx", "fsdp"), axis=0, tiled=True),
    )
    hidden_normed, pre_back = jax.vjp(normalize, hidden, gain_pre)
    hidden_low = hidden_normed.astype(jnp.bfloat16)
    gate_up = contract_last(hidden_low, gate_up_full)
    mixed, mix_back = jax.vjp(activate, gate_up)
    mixed_low = mixed.astype(jnp.bfloat16)
    down = jnp.dot(mixed_low, down_full, preferred_element_type=jnp.float32)
    down_normed, post_back = jax.vjp(normalize, down, gain_post)
    output = (hidden + down_normed).astype(jnp.bfloat16)
    gate_up_back, down_back = (
        lax.all_gather(gate_up_weight.astype(jnp.bfloat16), ("ctx", "fsdp"), axis=0, tiled=True),
        lax.all_gather(down_weight.astype(jnp.bfloat16), ("ctx", "fsdp"), axis=0, tiled=True),
    )
    grad_rows = cotangent[0].astype(jnp.float32)
    grad_down, grad_gain_post = post_back(grad_rows)
    grad_down_low = grad_down.astype(jnp.bfloat16)
    down_grad = contract_first(mixed_low, grad_down_low)
    grad_mixed = contract_last(grad_down_low, down_back)
    (grad_gate_up,) = mix_back(grad_mixed)
    grad_gate_up_low = grad_gate_up.astype(jnp.bfloat16)
    gate_up_grad = contract_first(grad_gate_up_low, hidden_low)
    grad_hidden_low = jnp.dot(grad_gate_up_low, gate_up_back, preferred_element_type=jnp.float32)
    grad_from_pre, grad_gain_pre = pre_back(grad_hidden_low)
    grad_hidden = grad_rows + grad_from_pre
    gate_up_part, down_part = (
        lax.psum_scatter(gate_up_grad, ("ctx", "fsdp"), scatter_dimension=0, tiled=True),
        lax.psum_scatter(down_grad, ("ctx", "fsdp"), scatter_dimension=0, tiled=True),
    )
    qkv_back, out_back = (
        lax.all_gather(qkv_weight.astype(jnp.bfloat16), ("ctx", "fsdp"), axis=0, tiled=True),
        lax.all_gather(out_weight.astype(jnp.bfloat16), ("ctx", "fsdp"), axis=0, tiled=True),
    )
    grad_branch, grad_gain_attend = attend_back(grad_hidden)
    grad_branch_low = grad_branch.astype(jnp.bfloat16)
    out_grad = contract_first(attended, grad_branch_low)
    grad_attended = (
        contract_last(grad_branch_low, out_back).astype(jnp.bfloat16).reshape(rows, H, HD)
    )
    scores_again = (
        jnp.einsum("thd,ld->thl", query, keys, preferred_element_type=jnp.float32) * scale
    )
    probs = jnp.exp(jnp.where(allowed, scores_again, -1e30) - log_total)
    grad_probs = jnp.einsum(
        "thd,ld->thl", grad_attended, values, preferred_element_type=jnp.float32
    )
    row_term = jnp.sum(probs * grad_probs, axis=-1, keepdims=True)
    grad_scores = (probs * (grad_probs - row_term)).astype(jnp.bfloat16)
    grad_query = (
        jnp.einsum("thl,ld->thd", grad_scores, keys, preferred_element_type=jnp.float32) * scale
    )
    grad_keys = (
        jnp.einsum("thl,thd->ld", grad_scores, query, preferred_element_type=jnp.float32) * scale
    )
    grad_values = jnp.einsum(
        "thl,thd->ld", probs.astype(jnp.bfloat16), grad_attended, preferred_element_type=jnp.float32
    )
    empty = jnp.zeros((front + length, HD), jnp.float32)
    keys_spread = lax.dynamic_update_slice_in_dim(empty, grad_keys, first_row, 0)[front:]
    values_spread = lax.dynamic_update_slice_in_dim(empty, grad_values, first_row, 0)[front:]
    grad_key, grad_value = (
        lax.psum_scatter(keys_spread, "ctx", scatter_dimension=0, tiled=True),
        lax.psum_scatter(values_spread, "ctx", scatter_dimension=0, tiled=True),
    )
    grad_proj_query, grad_proj_key, grad_gain_query, grad_gain_key = rotate_back(
        (grad_query, grad_key)
    )
    grad_projected = jnp.concatenate(
        [grad_proj_query.reshape(rows, query_width), grad_proj_key, grad_value], axis=1
    ).astype(jnp.bfloat16)
    qkv_grad = contract_first(grad_projected, normed_low)
    grad_normed = jnp.dot(grad_projected, qkv_back, preferred_element_type=jnp.float32)
    grad_from_input, grad_gain_input = input_back(grad_normed)
    input_grad = grad_hidden + grad_from_input
    gains_grad = jnp.concatenate(
        [
            grad_gain_input,
            grad_gain_attend,
            grad_gain_pre,
            grad_gain_post,
            grad_gain_query,
            grad_gain_key,
        ]
    )
    qkv_part, out_part, gains_part = (
        lax.psum_scatter(qkv_grad, ("ctx", "fsdp"), scatter_dimension=0, tiled=True),
        lax.psum_scatter(out_grad, ("ctx", "fsdp"), scatter_dimension=0, tiled=True),
        lax.psum_scatter(gains_grad, ("ctx", "fsdp"), scatter_dimension=0, tiled=True),
    )
    qkv_total, out_total, gate_up_total, down_total, gains_total = (
        lax.psum(qkv_part.astype(jnp.bfloat16), "dp").astype(jnp.float32),
        lax.psum(out_part.astype(jnp.bfloat16), "dp").astype(jnp.float32),
        lax.psum(gate_up_part.astype(jnp.bfloat16), "dp").astype(jnp.float32),
        lax.psum(down_part.astype(jnp.bfloat16), "dp").astype(jnp.float32),
        lax.psum(gains_part.astype(jnp.bfloat16), "dp").astype(jnp.float32),
    )
    qkv_new, qkv_first_new, qkv_second_new = adamw(qkv_weight, qkv_total, qkv_first, qkv_second)
    out_new, out_first_new, out_second_new = adamw(out_weight, out_total, out_first, out_second)
    gate_up_new, gate_up_first_new, gate_up_second_new = adamw(
        gate_up_weight, gate_up_total, gate_up_first, gate_up_second
    )
    down_new, down_first_new, down_second_new = adamw(
        down_weight, down_total, down_first, down_second
    )
    gains_new, gains_first_new, gains_second_new = adamw(
        gains, gains_total, gains_first, gains_second
    )
    return (
        output[None],
        input_grad[None],
        qkv_total,
        out_total,
        gate_up_total,
        down_total,
        gains_total,
        qkv_new,
        out_new,
        gate_up_new,
        down_new,
        gains_new,
        qkv_first_new,
        out_first_new,
        gate_up_first_new,
        down_first_new,
        gains_first_new,
        qkv_second_new,
        out_second_new,
        gate_up_second_new,
        down_second_new,
        gains_second_new,
    )


def solution(mesh):
    in_specs = (
        P(("dp", "fsdp"), "ctx", None),
        P(("dp", "fsdp"), "ctx", None),
        P(("dp", "fsdp"), None),
        P(("ctx", "fsdp"), None),
        P(("ctx", "fsdp"), None),
        P(("ctx", "fsdp"), None),
        P(("ctx", "fsdp"), None),
        P(("ctx", "fsdp")),
        P(("ctx", "fsdp"), None),
        P(("ctx", "fsdp"), None),
        P(("ctx", "fsdp"), None),
        P(("ctx", "fsdp"), None),
        P(("ctx", "fsdp")),
        P(("ctx", "fsdp"), None),
        P(("ctx", "fsdp"), None),
        P(("ctx", "fsdp"), None),
        P(("ctx", "fsdp"), None),
        P(("ctx", "fsdp")),
    )
    out_specs = (
        P(("dp", "fsdp"), "ctx", None),
        P(("dp", "fsdp"), "ctx", None),
        P(("ctx", "fsdp"), None),
        P(("ctx", "fsdp"), None),
        P(("ctx", "fsdp"), None),
        P(("ctx", "fsdp"), None),
        P(("ctx", "fsdp")),
        P(("ctx", "fsdp"), None),
        P(("ctx", "fsdp"), None),
        P(("ctx", "fsdp"), None),
        P(("ctx", "fsdp"), None),
        P(("ctx", "fsdp")),
        P(("ctx", "fsdp"), None),
        P(("ctx", "fsdp"), None),
        P(("ctx", "fsdp"), None),
        P(("ctx", "fsdp"), None),
        P(("ctx", "fsdp")),
        P(("ctx", "fsdp"), None),
        P(("ctx", "fsdp"), None),
        P(("ctx", "fsdp"), None),
        P(("ctx", "fsdp"), None),
        P(("ctx", "fsdp")),
    )
    return jax.shard_map(body, mesh=mesh, in_specs=in_specs, out_specs=out_specs, check_vma=False)
```

profile of v0, /device:TPU:0, one launch (start us, length us, event | category | flops | bytes accessed | tf_op | source)
XLA Modules:
  0.0 2683.0 jit_solution(189627027710603914)
XLA Ops:
  7.2 1.7 convert_element_type.117
  9.0 1.6 convert_element_type.122
  10.8 3.7 convert_element_type.124
  14.6 1.1 convert_element_type.126
  17.3 79.4 %all-reduce.9 = bf16[5120]{0:T(1024)(128)(2,1)S(1)} all-reduce(bf16[5120]{0:T(1024)(128)(2,1)S(1)} %dynamic-update-slice), channel_id=1, replica_groups=mesh['dp'=2,'ctx'=8,'fsdp'=2] {'ctx','fsdp'}, use_global_device_ids=true, to_apply=%add.9 | all-reduce | flops 5120 | bytes 20480
  97.9 0.8 compare_and_fusion
  98.7 3.3 fusion.60
  103.2 31.8 %all_gather.27 = bf16[1024,256]{1,0:T(8,128)(2,1)S(1)} all-gather(bf16[128,256]{1,0:T(8,128)(2,1)S(1)} %pad_maximum_fusion.6), channel_id=1, replica_groups=mesh['dp'=2,'ctx'=8,'fsdp'=2] {'ctx'}, dimensions={0}, use_global_device_ids=true | all-gather | bytes 589824 | tf_op jit(solution)/shard_map/all_gather | solution.py:136
  135.3 1.7 fusion.98
  137.5 32.5 %all_gather.28 = bf16[1024,256]{1,0:T(8,128)(2,1)S(1)} all-gather(bf16[128,256]{1,0:T(8,128)(2,1)S(1)} %slice.142), channel_id=1, replica_groups=mesh['dp'=2,'ctx'=8,'fsdp'=2] {'ctx'}, dimensions={0}, use_global_device_ids=true | all-gather | bytes 589824 | tf_op jit(solution)/shard_map/all_gather | solution.py:137
  170.9 2.3 multiply_reduce_fusion.7
  173.6 318.3 %all-gather.9.cloned.1.call-done = bf16[13824,1152]{1,0:T(8,128)(2,1)} async-done(((bf16[864,1152]{1,0:T(8,128)(2,1)}), bf16[13824,1152]{1,0:T(8,128)(2,1)}) %all-gather.9.cloned.1.call-update) | async-done | bytes 31850512 | tf_op jit(solution)/shard_map/all_gather | solution.py:153
  491.9 18.4 fusion.91
  510.3 4.3 multiply_convert_fusion
  514.6 162.3 %all-gather.11.cloned.1.call-done = bf16[6912,1152]{1,0:T(8,128)(2,1)} async-done(((bf16[432,1152]{1,0:T(8,128)(2,1)}), bf16[6912,1152]{1,0:T(8,128)(2,1)}) %all-gather.11.cloned.1.call-update) | async-done | bytes 15925264 | tf_op jit(solution)/shard_map/all_gather | solution.py:154
  677.0 8.1 multiply_reduce_fusion.5
  685.1 0.8 fusion.24
  685.9 1.0 fusion.20
  686.9 12.4 fusion.11
  699.3 18.4 multiply_reduce_fusion.1
  717.7 2.7 multiply_reduce_fusion.2
  720.4 0.8 copy-done.13
  721.2 1.2 fusion.21
  722.4 0.9 convolution_convert_fusion
  724.1 1.0 slice.105
  725.2 1.5 multiply_reduce_fusion
  728.1 1.0 slice.104
  729.2 2.9 fusion.99
  732.2 1.0 copy-done.17
  733.2 1.2 convolution_multiply_fusion
  735.7 51.3 %reduce-scatter.9.cloned.1.call-done = f32[128,256]{1,0:T(8,128)} async-done(((f32[1024,256]{1,0:T(8,128)}), f32[128,256]{1,0:T(8,128)}) %reduce-scatter.9.cloned.1.call-update) | async-done | bytes 131088 | tf_op jit(solution)/shard_map/reduce_scatter | solution.py:216
  787.0 0.9 convert.34
  788.0 65.7 %reduce-scatter.7.cloned.1.call-done = f32[128,256]{1,0:T(8,128)} async-done(((f32[1024,256]{1,0:T(8,128)}), f32[128,256]{1,0:T(8,128)}) %reduce-scatter.7.cloned.1.call-update) | async-done | bytes 131088 | tf_op jit(solution)/shard_map/reduce_scatter | solution.py:215
  853.7 1.2 fusion.66
  854.9 1.6 multiply_reduce_fusion.10
  857.2 1.0 fusion.50
  858.4 4.0 fusion.48
  862.5 0.9 copy-done.30
  863.4 12.9 fusion.100
  876.4 1.0 copy-done.2
  877.4 26.9 %fusion.29 = f32[13824,1152]{1,0:T(8,128)} fusion(f32[128,6912]{1,0:T(8,128)} %get-tuple-element.62, f32[128,6912]{1,0:T(8,128)} %get-tuple-element.61, f32[128,1152]{1,0:T(8,128)S(1)} %copy-done.2, f32[1152]{0:T(1024)S(1)} %get-tuple-element.74, f32[128]{0:T(128)S(1)} %fusion.79), kind=kOutput, calls=%fused_computation.81 | convolution fusion | flops 4080844800 | bytes 71373824 | tf_op jit(solution)/shard_map/dot_general | solution.py:44
  904.3 91.1 %reduce-scatter.13.cloned.1.call-done = f32[64,1152]{1,0:T(8,128)} async-done(((f32[1024,1152]{1,0:T(8,128)}), f32[64,1152]{1,0:T(8,128)}) %reduce-scatter.13.cloned.1.call-update) | async-done | bytes 294928 | tf_op jit(solution)/shard_map/reduce_scatter | solution.py:240
  995.5 1.6 convert_element_type.137
  997.1 154.8 %reduce-scatter.11.cloned.1.call-done = f32[96,1152]{1,0:T(8,128)} async-done(((f32[1536,1152]{1,0:T(8,128)}), f32[96,1152]{1,0:T(8,128)}) %reduce-scatter.11.cloned.1.call-update) | async-done | bytes 442384 | tf_op jit(solution)/shard_map/reduce_scatter | solution.py:239
  1152.0 1.7 convert_element_type.135
  1153.7 483.3 %reduce-scatter.17.cloned.1.call-done = f32[432,1152]{1,0:T(8,128)} async-done(((f32[6912,1152]{1,0:T(8,128)}), f32[432,1152]{1,0:T(8,128)}) %reduce-scatter.17.cloned.1.call-update) | async-done | bytes 1990672 | tf_op jit(solution)/shard_map/reduce_scatter | solution.py:181
  1637.0 2.6 convert_element_type.141
  1639.6 920.1 %reduce-scatter.15.cloned.1.call-done = f32[864,1152]{1,0:T(8,128)} async-done(((f32[13824,1152]{1,0:T(8,128)}), f32[864,1152]{1,0:T(8,128)}) %reduce-scatter.15.cloned.1.call-update) | async-done | bytes 3981328 | tf_op jit(solution)/shard_map/reduce_scatter | solution.py:180
  2559.7 3.6 convert_element_type.139
  2564.0 3.2 fusion.18
  2567.3 1.4 constant_dynamic-update-slice_fusion.5
  2568.7 1.3 constant_dynamic-update-slice_fusion.4
  2570.0 1.3 constant_dynamic-update-slice_fusion.3
  2571.3 1.3 constant_dynamic-update-slice_fusion.2
  2572.6 1.3 constant_dynamic-update-slice_fusion.1
  2573.9 1.3 constant_dynamic-update-slice_fusion
  2575.2 75.5 %all-reduce.10 = bf16[5120]{0:T(1024)(128)(2,1)S(1)} all-reduce(f32[5120]{0:T(1024)} %constant_dynamic-update-slice_fusion), channel_id=8, replica_groups=mesh['dp'=2,'ctx'=8,'fsdp'=2] {'ctx','fsdp'}, use_global_device_ids=true, to_apply=%region_33.34.clone | all-reduce | flops 5120 | bytes 30720
  2650.7 2.4 psum.39
  2653.9 1.3 multiply_subtract_fusion.4
  2655.2 2.3 fusion.23
  2657.5 2.8 multiply_subtract_fusion.2
  2660.3 2.0 multiply_subtract_fusion.3
  2662.3 10.2 multiply_subtract_fusion
  2672.6 3.6 multiply_subtract_fusion.1
  (200 shorter events, 10.7 us)
Async XLA Ops:
  7.2 91.5 %all-gather.5.cloned.1.call-start = ((), (), s32[]{:S(2)}) async-start(), calls=%async_computation.6 | async-start | bytes 3760128 | tf_op jit(solution)/shard_map/all_gather | solution.py:92
  9.0 161.9 %all-gather.7.cloned.1.call-start = ((), (), s32[]{:S(2)}) async-start(), calls=%async_computation.7 | async-start | bytes 2506752 | tf_op jit(solution)/shard_map/all_gather | solution.py:93
  10.7 3.9 copy-start.11
  10.7 481.2 %all-gather.9.cloned.1.call-start = ((), (), s32[]{:S(2)}) async-start(), calls=%async_computation.8 | async-start | bytes 33841152 | tf_op jit(solution)/shard_map/all_gather | solution.py:153
  14.5 1.2 copy-start.48
  14.5 1.3 copy-start.56
  14.5 82.2 %copy-start.40 = (s32[1,1024]{1,0:T(1,128)S(1)}, s32[1,1024]{1,0:T(1,128)}, u32[]{:S(2)}) copy-start(s32[1,1024]{1,0:T(1,128)} %param.20) | copy-start | bytes 12292
  14.5 83.1 %copy-start.7 = (bf16[1,128,1152]{2,1,0:T(8,128)(2,1)S(1)}, bf16[1,128,1152]{2,1,0:T(8,128)(2,1)}, u32[]{:S(2)}) copy-start(bf16[1,128,1152]{2,1,0:T(8,128)(2,1)} %param.18) | copy-start | bytes 884740
  14.5 662.4 %all-gather.11.cloned.1.call-start = ((), (), s32[]{:S(2)}) async-start(), calls=%async_computation.9 | async-start | bytes 16920576 | tf_op jit(solution)/shard_map/all_gather | solution.py:154
  15.7 771.3 %reduce-scatter.9.cloned.1.call-start = ((), (), s32[]{:S(2)}) async-start(), calls=%async_computation.11 | async-start | bytes 1179648 | tf_op jit(solution)/shard_map/reduce_scatter | solution.py:216
  97.5 5.3 copy-start.54
  97.5 5.3 copy-start.55
  97.8 4.7 copy-start.57
  97.8 4.7 copy-start.49
  97.8 4.9 copy-start.44
  97.9 37.2 %copy-start.46 = (f32[256]{0:T(256)}, f32[256]{0:T(256)S(1)}, u32[]{:S(2)}) copy-start(f32[256]{0:T(256)S(1)} %get-tuple-element.77) | copy-start | bytes 3076
  102.0 35.1 %copy-start.15 = (f32[128,1536]{1,0:T(8,128)}, f32[128,1536]{1,0:T(8,128)S(1)}, u32[]{:S(2)}) copy-start(f32[128,1536]{1,0:T(8,128)S(1)} %fusion.60) | copy-start | bytes 2359300
  102.0 35.0 %copy-start.5 = (f32[128,1024]{1,0:T(8,128)}, f32[128,1024]{1,0:T(8,128)S(1)}, u32[]{:S(2)}) copy-start(f32[128,1024]{1,0:T(8,128)S(1)} %slice.89) | copy-start | bytes 1572868
  102.7 34.4 %copy-start.58 = (f32[128]{0:T(128)}, f32[128]{0:T(128)S(1)}, u32[]{:S(2)}) copy-start(f32[128]{0:T(128)S(1)} %multiply_reduce_fusion.12) | copy-start | bytes 1540
  102.7 32.6 %copy-start.51 = (f32[128]{0:T(128)}, f32[128]{0:T(128)S(1)}, u32[]{:S(2)}) copy-start(f32[128]{0:T(128)S(1)} %fusion.77) | copy-start | bytes 1540
  135.1 2.0 copy-start.25
  135.3 1.8 copy-start.36
  135.3 1.8 copy-start.38
  170.9 321.0 %copy-start.22 = (bf16[128,4,256]{0,2,1:T(8,128)(2,1)}, bf16[128,4,256]{0,2,1:T(8,128)(2,1)S(1)}, u32[]{:S(2)}) copy-start(bf16[128,4,256]{0,2,1:T(8,128)(2,1)S(1)} %copy.88) | copy-start | bytes 786436
  173.3 318.6 %copy-start.10 = (f32[128,1152]{1,0:T(8,128)}, f32[128,1152]{1,0:T(8,128)S(1)}, u32[]{:S(2)}) copy-start(f32[128,1152]{1,0:T(8,128)S(1)} %get-tuple-element.86) | copy-start | bytes 1769476
  173.6 318.3 %copy-start = (f32[128,1152]{1,0:T(8,128)}, f32[128,1152]{1,0:T(8,128)S(1)}, u32[]{:S(2)}) copy-start(f32[128,1152]{1,0:T(8,128)S(1)} %get-tuple-element.60) | copy-start | bytes 1769476
  677.0 8.2 copy-start.18
  677.0 9.0 copy-start.1
  686.9 12.4 copy-start.29
  717.7 4.7 copy-start.9
  722.4 1.7 copy-start.19
  725.2 128.5 %reduce-scatter.7.cloned.1.call-start = ((), (), s32[]{:S(2)}) async-start(), calls=%async_computation.10 | async-start | bytes 1179648 | tf_op jit(solution)/shard_map/reduce_scatter | solution.py:215
  727.1 1.0 copy-start.16
  727.1 2.1 copy-start.20
  727.1 2.1 copy-start.23
  729.2 266.3 %reduce-scatter.13.cloned.1.call-start = ((), (), s32[]{:S(2)}) async-start(), calls=%async_computation.13 | async-start | bytes 5013504 | tf_op jit(solution)/shard_map/reduce_scatter | solution.py:240
  732.1 1.1 copy-start.17
  732.1 2.4 copy-start.6
  732.1 2.4 copy-start.47
  732.1 122.8 %copy-start.45 = (f32[256]{0:T(256)S(1)}, f32[256]{0:T(256)}, u32[]{:S(2)}) copy-start(f32[256]{0:T(256)} %copy-done.44) | copy-start | bytes 3076
  732.2 126.2 %copy-start.8 = (bf16[1,128,1152]{2,1,0:T(8,128)(2,1)S(1)}, bf16[1,128,1152]{2,1,0:T(8,128)(2,1)}, u32[]{:S(2)}) copy-start(bf16[1,128,1152]{2,1,0:T(8,128)(2,1)} %param.18) | copy-start | bytes 884740
  732.2 126.2 %copy-start.50 = (f32[128]{0:T(128)S(1)}, f32[128]{0:T(128)}, u32[]{:S(2)}) copy-start(f32[128]{0:T(128)} %copy-done.49) | copy-start | bytes 1540
  732.2 419.8 %reduce-scatter.11.cloned.1.call-start = ((), (), s32[]{:S(2)}) async-start(), calls=%async_computation.12 | async-start | bytes 7520256 | tf_op jit(solution)/shard_map/reduce_scatter | solution.py:239
  735.7 126.7 %copy-start.24 = (bf16[128,4,256]{0,2,1:T(8,128)(2,1)}, bf16[128,4,256]{0,2,1:T(8,128)(2,1)S(1)}, u32[]{:S(2)}) copy-start(bf16[128,4,256]{0,2,1:T(8,128)(2,1)S(1)} %copy.92) | copy-start | bytes 786436
  788.0 74.4 %copy-start.32 = (bf16[128,256]{0,1:T(8,128)(2,1)}, bf16[128,256]{0,1:T(8,128)(2,1)S(1)}, u32[]{:S(2)}) copy-start(bf16[128,256]{0,1:T(8,128)(2,1)S(1)} %copy.97) | copy-start | bytes 196612
  858.3 4.1 copy-start.33
  862.4 774.5 %reduce-scatter.17.cloned.1.call-start = ((), (), s32[]{:S(2)}) async-start(), calls=%async_computation.15 | async-start | bytes 33841152 | tf_op jit(solution)/shard_map/reduce_scatter | solution.py:181
  876.3 1.1 copy-start.2
  876.3 1683.4 %reduce-scatter.15.cloned.1.call-start = ((), (), s32[]{:S(2)}) async-start(), calls=%async_computation.14 | async-start | bytes 67682304 | tf_op jit(solution)/shard_map/reduce_scatter | solution.py:180
  904.3 1753.2 %all-reduce.14.cloned.1.call-start = ((), (), s32[]{:S(2)}) async-start(), calls=%async_computation.16 | async-start | bytes 6709248 | tf_op jit(solution)/shard_map/psum | solution.py:244
  1639.6 924.4 %copy-start.4 = (bf16[1536,1152]{1,0:T(8,128)(2,1)S(1)}, bf16[1536,1152]{1,0:T(8,128)(2,1)}, u32[]{:S(2)}) copy-start(bf16[1536,1152]{1,0:T(8,128)(2,1)} %all-gather.5.cloned.1.call-done) | copy-start | bytes 10616836
  2563.3 8.0 copy-start.41
  2564.0 4.7 copy-start.42
  2564.0 6.0 copy-start.43
  2564.0 8.6 copy-start.53
  2564.0 9.9 copy-start.52
  2567.3 93.0 %copy-start.28 = (f32[64,1152]{1,0:T(8,128)S(1)}, f32[64,1152]{1,0:T(8,128)}, u32[]{:S(2)}) copy-start(f32[64,1152]{1,0:T(8,128)} %param.22) | copy-start | bytes 884740
  2567.3 93.0 %copy-start.34 = (f32[64,1152]{1,0:T(8,128)S(1)}, f32[64,1152]{1,0:T(8,128)}, u32[]{:S(2)}) copy-start(f32[64,1152]{1,0:T(8,128)} %param.27) | copy-start | bytes 884740
  2567.3 93.0 %copy-start.35 = (f32[64,1152]{1,0:T(8,128)S(1)}, f32[64,1152]{1,0:T(8,128)}, u32[]{:S(2)}) copy-start(f32[64,1152]{1,0:T(8,128)} %param.32) | copy-start | bytes 884740
  2657.5 4.8 copy-start.3
  2662.3 10.3 copy-start.12
  2662.3 10.3 copy-start.26
  2662.3 10.3 copy-start.27
  2662.3 10.3 copy-start.31
  (6 other events, 5.3 us)
Sparse Core Ops, SparseCore 0:
  11.4 74.5 all-gather.4
  89.4 64.6 all-gather.6
  157.5 334.3 all-gather.8
  495.1 181.8 all-gather.10
  725.3 61.6 reduce-scatter.8
  791.2 62.4 reduce-scatter.6
  858.9 136.5 reduce-scatter.12
  1001.7 150.2 reduce-scatter.10
  1159.0 477.8 reduce-scatter.16
  1643.9 915.7 reduce-scatter.14
  2564.0 23.4 all-reduce.13
where the time goes:
time: 2690 us; the launch traced here: 2680 us
  waiting for transfers between devices  2250 us (84%)
  blocking collectives  222 us (8%)
  matrix products  120 us (4%)
  other arithmetic  60.8 us (2%)
    reduce_scatter x1, waiting for transfers between devices, body(): lax.psum_scatter(gate_up_grad, ('ctx', 'fsdp'), scatter_dimension=0, tile...  920 us
    reduce_scatter x1, waiting for transfers between devices, body(): lax.psum_scatter(down_grad, ('ctx', 'fsdp'), scatter_dimension=0, tiled=T...  483 us
    all_gather x1, waiting for transfers between devices, body(): lax.all_gather(gate_up_weight.astype(jnp.bfloat16), ('ctx', 'fsdp'), axis...  318 us
    all_gather x1, waiting for transfers between devices, body(): lax.all_gather(down_weight.astype(jnp.bfloat16), ('ctx', 'fsdp'), axis=0,...  162 us
    unnamed x2, blocking collectives  155 us
    reduce_scatter x1, waiting for transfers between devices, body(): lax.psum_scatter(qkv_grad, ('ctx', 'fsdp'), scatter_dimension=0, tiled=True)  155 us
    reduce_scatter x1, waiting for transfers between devices, body(): lax.psum_scatter(out_grad, ('ctx', 'fsdp'), scatter_dimension=0, tiled=True)  91.1 us
    reduce_scatter x1, waiting for transfers between devices, body(): lax.psum_scatter(keys_spread, 'ctx', scatter_dimension=0, tiled=True)  65.7 us
  transfers between devices with their start and end apart: 11, of which 8 were waited for; matrix products, arithmetic and copies ran while one was open for 5% of the time, Pallas kernels for 0%

commit v1 on v0

--- a/solution.py
+++ b/solution.py
@@ -80,6 +80,29 @@
     down_second,
     gains_second,
 ):
+
+    def update_corner(here_x):
+        outcome_arr, out_arr, spare = (
+            lax.axis_size(("ctx", "fsdp")),
+            lax.axis_index(("ctx", "fsdp")),
+            here_x.shape[0],
+        )
+        finding, x_now = (here_x, 1)
+        while x_now < outcome_arr:
+            finding = jnp.concatenate(
+                [
+                    finding,
+                    lax.ppermute(
+                        finding,
+                        ("ctx", "fsdp"),
+                        [(idx, (idx - x_now) % outcome_arr) for idx in range(outcome_arr)],
+                    ),
+                ],
+                0,
+            )
+            x_now = 2 * x_now
+        return jnp.roll(finding, out_arr * spare, 0)
+
     rows = tokens.shape[1]
     width = tokens.shape[2]
     length = segments.shape[1]
@@ -151,7 +174,7 @@
     hidden = x_rows + branch_normed
     gate_up_full, down_full = (
         lax.all_gather(gate_up_weight.astype(jnp.bfloat16), ("ctx", "fsdp"), axis=0, tiled=True),
-        lax.all_gather(down_weight.astype(jnp.bfloat16), ("ctx", "fsdp"), axis=0, tiled=True),
+        update_corner(down_weight.astype(jnp.bfloat16)),
     )
     hidden_normed, pre_back = jax.vjp(normalize, hidden, gain_pre)
     hidden_low = hidden_normed.astype(jnp.bfloat16)

time: 2690 us -> 3140 us (1.17)
  blocking collectives: 222 us -> 550 us
  waiting for transfers between devices: 2250 us -> 2310 us
    unnamed x2, blocking collectives: 155 us -> 481 us
    ppermute x0 -> x4, waiting for transfers between devices: none -> 185 us  [update_corner(): lax.ppermute(finding, ('ctx', 'fsdp'), [(idx, (idx - x_now) % outcome_arr...]
    all_gather x1, waiting for transfers between devices: 318 us -> 204 us  [body(): lax.all_gather(gate_up_weight.astype(jnp.bfloat16), ('ctx', 'fsdp'), axis...]
  transfers between devices with their start and end apart: 11 -> 15, of which waited for: 8 -> 11; matrix products, arithmetic and copies ran while one was open for 5% -> 6% of each run, Pallas kernels for 0% -> 0%
where the time goes in v1:
time: 3140 us
  waiting for transfers between devices  2310 us (74%)
  blocking collectives  550 us (18%)
  matrix products  123 us (4%)
  other arithmetic  84.1 us (3%)
  local copies, waits for them, and re-layouts  46.4 us (1%)
    reduce_scatter x1, waiting for transfers between devices, body(): lax.psum_scatter(gate_up_grad, ('ctx', 'fsdp'), scatter_dimension=0, tile...  920 us
    reduce_scatter x1, waiting for transfers between devices, body(): lax.psum_scatter(down_grad, ('ctx', 'fsdp'), scatter_dimension=0, tiled=T...  484 us
    unnamed x2, blocking collectives  481 us
    all_gather x1, waiting for transfers between devices, body(): lax.all_gather(gate_up_weight.astype(jnp.bfloat16), ('ctx', 'fsdp'), axis...  204 us
    ppermute x4, waiting for transfers between devices, update_corner(): lax.ppermute(finding, ('ctx', 'fsdp'), [(idx, (idx - x_now) % outcome_arr...  185 us
    reduce_scatter x1, waiting for transfers between devices, body(): lax.psum_scatter(qkv_grad, ('ctx', 'fsdp'), scatter_dimension=0, tiled=True)  155 us
    all_gather x1, waiting for transfers between devices, body(): lax.all_gather(down_weight.astype(jnp.bfloat16), ('ctx', 'fsdp'), axis=0,...  149 us
    reduce_scatter x1, waiting for transfers between devices, body(): lax.psum_scatter(out_grad, ('ctx', 'fsdp'), scatter_dimension=0, tiled=True)  95.5 us
  transfers between devices with their start and end apart: 15, of which 11 were waited for; matrix products, arithmetic and copies ran while one was open for 6% of the time, Pallas kernels for 0%

profile of v1, /device:TPU:0, one launch (start us, length us, event | category | flops | bytes accessed | tf_op | source)
XLA Modules:
  0.0 3135.4 jit_solution(9215079062652213112)
XLA Ops:
  7.2 1.7 convert_element_type.117
  9.0 1.6 convert_element_type.122
  10.8 3.7 convert_element_type.124
  14.6 1.5 constant_dynamic-update-slice_fusion.9
  16.1 7.0 collective-permute-start
  23.1 26.3 collective-permute-done
  49.4 1.7 pad_maximum_fusion.2
  51.2 52.3 %collective-permute-done.1 = bf16[864,1152]{1,0:T(8,128)(2,1)S(1)} collective-permute-done((bf16[864,1152]{1,0:T(8,128)(2,1)S(1)}, bf16[864,1152]{1,0:T(8,128)(2,1)S(1)}, u32[]{:S(2)}, u32[]{:S(2)}) %collective-permute-start.1) | collective-permute-done | bytes 1990688 | tf_op jit(solution)/shard_map/ppermute | solution.py:95
  103.6 6.1 pad_maximum_fusion.1
  109.8 106.1 %collective-permute-done.2 = bf16[1728,1152]{1,0:T(8,128)(2,1)S(1)} collective-permute-done((bf16[1728,1152]{1,0:T(8,128)(2,1)S(1)}, bf16[1728,1152]{1,0:T(8,128)(2,1)S(1)}, u32[]{:S(2)}, u32[]{:S(2)}) %collective-permute-start.2) | collective-permute-done | bytes 3981344 | tf_op jit(solution)/shard_map/ppermute | solution.py:95
  215.9 18.3 pad_maximum_fusion
  235.8 405.6 %all-reduce.9 = bf16[5120]{0:T(1024)(128)(2,1)S(1)} all-reduce(bf16[5120]{0:T(1024)(128)(2,1)S(1)} %dynamic-update-slice), channel_id=1, replica_groups=mesh['dp'=2,'ctx'=8,'fsdp'=2] {'ctx','fsdp'}, use_global_device_ids=true, to_apply=%add.9 | all-reduce | flops 5120 | bytes 20480
  645.0 1.4 constant_dynamic-update-slice_fusion.7
  646.4 3.3 fusion.62
  651.7 33.0 %all_gather.26 = bf16[1024,256]{1,0:T(8,128)(2,1)S(1)} all-gather(bf16[128,256]{1,0:T(8,128)(2,1)S(1)} %pad_maximum_fusion.9), channel_id=1, replica_groups=mesh['dp'=2,'ctx'=8,'fsdp'=2] {'ctx'}, dimensions={0}, use_global_device_ids=true | all-gather | bytes 589824 | tf_op jit(solution)/shard_map/all_gather | solution.py:159
  685.0 1.7 fusion.101
  687.2 33.2 %all_gather.27 = bf16[1024,256]{1,0:T(8,128)(2,1)S(1)} all-gather(bf16[128,256]{1,0:T(8,128)(2,1)S(1)} %copy-done.44), channel_id=1, replica_groups=mesh['dp'=2,'ctx'=8,'fsdp'=2] {'ctx'}, dimensions={0}, use_global_device_ids=true | all-gather | bytes 589824 | tf_op jit(solution)/shard_map/all_gather | solution.py:160
  720.4 1.4 convolution_convert_fusion.1
  721.7 1.8 copy.88
  723.5 2.5 multiply_reduce_fusion.7
  726.9 2.2 constant_dynamic-update-slice_fusion.6
  729.1 7.1 constant_dynamic-update-slice_fusion.5
  737.3 2.3 constant_dynamic-update-slice_fusion.3
  739.5 1.5 constant_dynamic-update-slice_fusion.2
  741.0 2.2 constant_dynamic-update-slice_fusion.1
  743.2 7.1 constant_dynamic-update-slice_fusion
  750.3 203.9 %all-gather.9.cloned.1.call-done = bf16[13824,1152]{1,0:T(8,128)(2,1)} async-done(((bf16[864,1152]{1,0:T(8,128)(2,1)}), bf16[13824,1152]{1,0:T(8,128)(2,1)}) %all-gather.9.cloned.1.call-update) | async-done | bytes 31850512 | tf_op jit(solution)/shard_map/all_gather | solution.py:176
  954.2 18.7 fusion.94
  972.9 4.3 multiply_convert_fusion
  977.3 11.4 multiply_reduce_fusion.5
  990.4 148.9 %all-gather.11.cloned.1.call-done = bf16[6912,1152]{1,0:T(8,128)(2,1)} async-done(((bf16[432,1152]{1,0:T(8,128)(2,1)}), bf16[6912,1152]{1,0:T(8,128)(2,1)}) %all-gather.11.cloned.1.call-update) | async-done | bytes 15925264 | tf_op jit(solution)/shard_map/all_gather | solution.py:189
  1139.3 12.4 fusion.13
  1151.8 18.4 multiply_reduce_fusion.1
  1170.2 2.2 multiply_reduce_fusion.2
  1179.6 2.9 fusion.102
  1185.7 53.8 %reduce-scatter.7.cloned.1.call-done = f32[128,256]{1,0:T(8,128)} async-done(((f32[1024,256]{1,0:T(8,128)}), f32[128,256]{1,0:T(8,128)}) %reduce-scatter.7.cloned.1.call-update) | async-done | bytes 131088 | tf_op jit(solution)/shard_map/reduce_scatter | solution.py:238
  1240.7 1.6 multiply_reduce_fusion.10
  1243.5 62.8 %reduce-scatter.9.cloned.1.call-done = f32[128,256]{1,0:T(8,128)} async-done(((f32[1024,256]{1,0:T(8,128)}), f32[128,256]{1,0:T(8,128)}) %reduce-scatter.9.cloned.1.call-update) | async-done | bytes 131088 | tf_op jit(solution)/shard_map/reduce_scatter | solution.py:239
  1307.3 4.1 fusion.50
  1311.6 1.2 copy-done.12
  1312.8 12.7 fusion.103
  1325.6 26.7 fusion.31
  1352.4 95.5 %reduce-scatter.13.cloned.1.call-done = f32[64,1152]{1,0:T(8,128)} async-done(((f32[1024,1152]{1,0:T(8,128)}), f32[64,1152]{1,0:T(8,128)}) %reduce-scatter.13.cloned.1.call-update) | async-done | bytes 294928 | tf_op jit(solution)/shard_map/reduce_scatter | solution.py:263
  1447.9 1.6 convert_element_type.137
  1449.5 154.6 %reduce-scatter.11.cloned.1.call-done = f32[96,1152]{1,0:T(8,128)} async-done(((f32[1536,1152]{1,0:T(8,128)}), f32[96,1152]{1,0:T(8,128)}) %reduce-scatter.11.cloned.1.call-update) | async-done | bytes 442384 | tf_op jit(solution)/shard_map/reduce_scatter | solution.py:262
  1604.2 1.7 convert_element_type.135
  1605.9 483.6 %reduce-scatter.17.cloned.1.call-done = f32[432,1152]{1,0:T(8,128)} async-done(((f32[6912,1152]{1,0:T(8,128)}), f32[432,1152]{1,0:T(8,128)}) %reduce-scatter.17.cloned.1.call-update) | async-done | bytes 1990672 | tf_op jit(solution)/shard_map/reduce_scatter | solution.py:204
  2089.5 2.6 convert_element_type.141
  2092.1 920.2 %reduce-scatter.15.cloned.1.call-done = f32[864,1152]{1,0:T(8,128)} async-done(((f32[13824,1152]{1,0:T(8,128)}), f32[864,1152]{1,0:T(8,128)}) %reduce-scatter.15.cloned.1.call-update) | async-done | bytes 3981328 | tf_op jit(solution)/shard_map/reduce_scatter | solution.py:203
  3012.3 3.6 convert_element_type.139
  3016.7 3.2 fusion.20
  3019.9 1.3 constant_dynamic-update-slice_fusion.10
  3021.2 1.3 constant_dynamic-update-slice_fusion.15
  3022.5 1.3 constant_dynamic-update-slice_fusion.14
  3023.8 1.3 constant_dynamic-update-slice_fusion.11
  3025.1 1.3 constant_dynamic-update-slice_fusion.13
  3026.4 1.3 constant_dynamic-update-slice_fusion.12
  3027.7 75.5 %all-reduce.10 = bf16[5120]{0:T(1024)(128)(2,1)S(1)} all-reduce(f32[5120]{0:T(1024)} %constant_dynamic-update-slice_fusion.12), channel_id=8, replica_groups=mesh['dp'=2,'ctx'=8,'fsdp'=2] {'ctx','fsdp'}, use_global_device_ids=true, to_apply=%region_33.34.clone | all-reduce | flops 5120 | bytes 30720
  3103.3 2.4 psum.39
  3106.4 1.3 multiply_subtract_fusion.4
  3107.7 2.3 fusion.25
  3110.1 11.5 multiply_subtract_fusion
  3122.6 3.6 multiply_subtract_fusion.1
  3126.3 1.3 multiply_subtract_fusion.2
  (274 shorter events, 27.7 us)
Async XLA Ops:
  7.2 639.2 %all-gather.5.cloned.1.call-start = ((), (), s32[]{:S(2)}) async-start(), calls=%async_computation.6 | async-start | bytes 3760128 | tf_op jit(solution)/shard_map/all_gather | solution.py:115
  9.0 714.5 %all-gather.7.cloned.1.call-start = ((), (), s32[]{:S(2)}) async-start(), calls=%async_computation.7 | async-start | bytes 2506752 | tf_op jit(solution)/shard_map/all_gather | solution.py:116
  10.7 943.5 %all-gather.9.cloned.1.call-start = ((), (), s32[]{:S(2)}) async-start(), calls=%async_computation.8 | async-start | bytes 33841152 | tf_op jit(solution)/shard_map/all_gather | solution.py:176
  14.5 1124.8 %all-gather.11.cloned.1.call-start = ((), (), s32[]{:S(2)}) async-start(), calls=%async_computation.9 | async-start | bytes 16920576 | tf_op jit(solution)/shard_map/all_gather | solution.py:189
  16.0 87.5 %copy-start.2 = (bf16[432,1152]{1,0:T(8,128)(2,1)S(1)}, bf16[432,1152]{1,0:T(8,128)(2,1)}, u32[]{:S(2)}) copy-start(bf16[432,1152]{1,0:T(8,128)(2,1)} %get-tuple-element.60) | copy-start | bytes 2985988
  16.1 1223.4 %reduce-scatter.7.cloned.1.call-start = ((), (), s32[]{:S(2)}) async-start(), calls=%async_computation.10 | async-start | bytes 1179648 | tf_op jit(solution)/shard_map/reduce_scatter | solution.py:238
  16.1 33.3 %collective-permute-start = (bf16[432,1152]{1,0:T(8,128)(2,1)}, bf16[432,1152]{1,0:T(8,128)(2,1)S(1)}, u32[]{:S(2)}, u32[]{:S(2)}) collective-permute-start(bf16[432,1152]{1,0:T(8,128)(2,1)} %get-tuple-element.60), channel_id=1, source_target_pairs={{0,15},{1,0},{2,1},{3,2},{4,3},{5,4},{6,5},{7,6},{8,7},{9,8},{10,9... | collective-permute-start | bytes 2985992 | tf_op jit(solution)/shard_map/ppermute | solution.py:95
  49.4 594.5 %copy-start.6 = (bf16[432,1152]{1,0:T(8,128)(2,1)}, bf16[432,1152]{1,0:T(8,128)(2,1)S(1)}, u32[]{:S(2)}) copy-start(bf16[432,1152]{1,0:T(8,128)(2,1)S(1)} %collective-permute-done) | copy-start | bytes 2985988
  51.2 52.4 %collective-permute-start.1 = (bf16[864,1152]{1,0:T(8,128)(2,1)S(1)}, bf16[864,1152]{1,0:T(8,128)(2,1)S(1)}, u32[]{:S(2)}, u32[]{:S(2)}) collective-permute-start(bf16[864,1152]{1,0:T(8,128)(2,1)S(1)} %pad_maximum_fusion.2), channel_id=1, source_target_pairs={{0,14},{1,15},{2,0},{3,1},{4,2},{5,3},{6,4},{7,5},{8,6},{9,7},{10,... | collective-permute-start | bytes 5971976 | tf_op jit(solution)/shard_map/ppermute | solution.py:95
  103.6 112.3 %copy-start.3 = (bf16[864,1152]{1,0:T(8,128)(2,1)}, bf16[864,1152]{1,0:T(8,128)(2,1)S(1)}, u32[]{:S(2)}) copy-start(bf16[864,1152]{1,0:T(8,128)(2,1)S(1)} %collective-permute-done.1) | copy-start | bytes 5971972
  109.7 124.5 %copy-start.65 = (f32[320]{0:T(512)S(1)}, f32[320]{0:T(512)}, u32[]{:S(2)}) copy-start(f32[320]{0:T(512)} %param.25) | copy-start | bytes 3844
  109.7 124.5 %copy-start.78 = (u32[32]{0:T(128)S(1)}, u32[32]{0:T(128)}, u32[]{:S(2)}) copy-start(u32[32]{0:T(128)} %constant.188) | copy-start | bytes 388
  109.7 531.7 %copy-start.53 = (s32[1,1024]{1,0:T(1,128)S(1)}, s32[1,1024]{1,0:T(1,128)}, u32[]{:S(2)}) copy-start(s32[1,1024]{1,0:T(1,128)} %param.20) | copy-start | bytes 12292
  109.7 532.7 %copy-start.10 = (bf16[1,128,1152]{2,1,0:T(8,128)(2,1)S(1)}, bf16[1,128,1152]{2,1,0:T(8,128)(2,1)}, u32[]{:S(2)}) copy-start(bf16[1,128,1152]{2,1,0:T(8,128)(2,1)} %param.18) | copy-start | bytes 884740
  109.7 106.2 %collective-permute-start.2 = (bf16[1728,1152]{1,0:T(8,128)(2,1)S(1)}, bf16[1728,1152]{1,0:T(8,128)(2,1)S(1)}, u32[]{:S(2)}, u32[]{:S(2)}) collective-permute-start(bf16[1728,1152]{1,0:T(8,128)(2,1)S(1)} %pad_maximum_fusion.1), channel_id=1, source_target_pairs={{0,12},{1,13},{2,14},{3,15},{4,0},{5,1},{6,2},{7,3},{8,4},{9,5},{1... | collective-permute-start | bytes 11943944 | tf_op jit(solution)/shard_map/ppermute | solution.py:95
  215.9 18.3 copy-start
  234.2 494.9 %collective-permute-start.3 = (bf16[3456,1152]{1,0:T(8,128)(2,1)}, bf16[3456,1152]{1,0:T(8,128)(2,1)}, u32[]{:S(2)}, u32[]{:S(2)}) collective-permute-start(bf16[3456,1152]{1,0:T(8,128)(2,1)} %pad_maximum_fusion), channel_id=1, source_target_pairs={{0,8},{1,9},{2,10},{3,11},{4,12},{5,13},{6,14},{7,15},{8,0},{9,1},... | collective-permute-start | bytes 23887880 | tf_op jit(solution)/shard_map/ppermute | solution.py:95
  642.3 9.0 copy-start.74
  642.3 9.0 copy-start.76
  643.1 6.6 copy-start.66
  643.1 8.1 copy-start.61
  643.1 41.6 %copy-start.63 = (f32[256]{0:T(256)}, f32[256]{0:T(256)S(1)}, u32[]{:S(2)}) copy-start(f32[256]{0:T(256)S(1)} %get-tuple-element.79) | copy-start | bytes 3076
  649.7 35.3 %copy-start.21 = (f32[128,1536]{1,0:T(8,128)}, f32[128,1536]{1,0:T(8,128)S(1)}, u32[]{:S(2)}) copy-start(f32[128,1536]{1,0:T(8,128)S(1)} %fusion.62) | copy-start | bytes 2359300
  649.8 36.9 %copy-start.8 = (f32[128,1024]{1,0:T(8,128)}, f32[128,1024]{1,0:T(8,128)S(1)}, u32[]{:S(2)}) copy-start(f32[128,1024]{1,0:T(8,128)S(1)} %slice.89) | copy-start | bytes 1572868
  651.0 33.9 %copy-start.59 = (f32[128,4]{0,1:T(4,128)}, f32[128,4]{0,1:T(4,128)S(1)}, u32[]{:S(2)}) copy-start(f32[128,4]{0,1:T(4,128)S(1)} %copy.86) | copy-start | bytes 6148
  651.2 33.8 %copy-start.82 = (f32[128]{0:T(128)}, f32[128]{0:T(128)S(1)}, u32[]{:S(2)}) copy-start(f32[128]{0:T(128)S(1)} %multiply_reduce_fusion.12) | copy-start | bytes 1540
  651.2 33.8 %copy-start.70 = (f32[128]{0:T(128)}, f32[128]{0:T(128)S(1)}, u32[]{:S(2)}) copy-start(f32[128]{0:T(128)S(1)} %fusion.80) | copy-start | bytes 1540
  651.6 33.3 %copy-start.38 = (f32[128,128]{1,0:T(8,128)}, f32[128,128]{1,0:T(8,128)S(1)}, u32[]{:S(2)}) copy-start(f32[128,128]{1,0:T(8,128)S(1)} %get-tuple-element.82) | copy-start | bytes 196612
  651.7 35.5 %copy-start.44 = (bf16[128,256]{1,0:T(8,128)(2,1)S(1)}, bf16[128,256]{1,0:T(8,128)(2,1)}, u32[]{:S(2)}) copy-start(bf16[128,256]{1,0:T(8,128)(2,1)} %slice.142) | copy-start | bytes 196612
  651.7 35.0 %copy-start.54 = (f32[128,4]{0,1:T(4,128)}, f32[128,4]{0,1:T(4,128)S(1)}, u32[]{:S(2)}) copy-start(f32[128,4]{0,1:T(4,128)S(1)} %fusion.72) | copy-start | bytes 6148
  687.2 39.7 %copy-start.51 = (f32[128,4]{0,1:T(4,128)}, f32[128,4]{0,1:T(4,128)S(1)}, u32[]{:S(2)}) copy-start(f32[128,4]{0,1:T(4,128)S(1)} %log_add_fusion) | copy-start | bytes 6148
  720.4 5.7 copy-start.19
  977.2 11.4 copy-start.11
  977.2 11.4 copy-start.24
  990.4 161.3 %copy-start.33 = (bf16[128,1152]{1,0:T(8,128)(2,1)}, bf16[128,1152]{1,0:T(8,128)(2,1)S(1)}, u32[]{:S(2)}) copy-start(bf16[128,1152]{1,0:T(8,128)(2,1)S(1)} %get-tuple-element.69) | copy-start | bytes 884740
  1151.7 18.4 copy-start.80
  1151.7 18.4 copy-start.15
  1151.7 18.4 copy-start.69
  1151.7 20.7 copy-start.85
  1177.6 128.6 %reduce-scatter.9.cloned.1.call-start = ((), (), s32[]{:S(2)}) async-start(), calls=%async_computation.11 | async-start | bytes 1179648 | tf_op jit(solution)/shard_map/reduce_scatter | solution.py:239
  1179.5 268.4 %reduce-scatter.13.cloned.1.call-start = ((), (), s32[]{:S(2)}) async-start(), calls=%async_computation.13 | async-start | bytes 5013504 | tf_op jit(solution)/shard_map/reduce_scatter | solution.py:263
  1182.5 56.9 %copy-start.75 = (f32[128]{0:T(128)S(1)}, f32[128]{0:T(128)}, u32[]{:S(2)}) copy-start(f32[128]{0:T(128)} %copy-done.74) | copy-start | bytes 1540
  1182.6 56.9 %copy-start.77 = (f32[128]{0:T(128)S(1)}, f32[128]{0:T(128)}, u32[]{:S(2)}) copy-start(f32[128]{0:T(128)} %copy-done.76) | copy-start | bytes 1540
  1182.6 58.1 %copy-start.62 = (f32[256]{0:T(256)S(1)}, f32[256]{0:T(256)}, u32[]{:S(2)}) copy-start(f32[256]{0:T(256)} %copy-done.61) | copy-start | bytes 3076
  1182.6 58.1 %copy-start.71 = (f32[128]{0:T(128)S(1)}, f32[128]{0:T(128)}, u32[]{:S(2)}) copy-start(f32[128]{0:T(128)} %copy-done.70) | copy-start | bytes 1540
  1182.6 59.7 %copy-start.83 = (f32[128]{0:T(128)S(1)}, f32[128]{0:T(128)}, u32[]{:S(2)}) copy-start(f32[128]{0:T(128)} %copy-done.82) | copy-start | bytes 1540
  1182.6 124.7 %copy-start.67 = (f32[128]{0:T(128)S(1)}, f32[128]{0:T(128)}, u32[]{:S(2)}) copy-start(f32[128]{0:T(128)} %copy-done.66) | copy-start | bytes 1540
  1182.6 421.6 %reduce-scatter.11.cloned.1.call-start = ((), (), s32[]{:S(2)}) async-start(), calls=%async_computation.12 | async-start | bytes 7520256 | tf_op jit(solution)/shard_map/reduce_scatter | solution.py:262
  1185.7 125.6 %copy-start.26 = (bf16[128,4,256]{0,2,1:T(8,128)(2,1)}, bf16[128,4,256]{0,2,1:T(8,128)(2,1)S(1)}, u32[]{:S(2)}) copy-start(bf16[128,4,256]{0,2,1:T(8,128)(2,1)S(1)} %copy.92) | copy-start | bytes 786436
  1243.4 67.9 %copy-start.36 = (bf16[128,256]{0,1:T(8,128)(2,1)}, bf16[128,256]{0,1:T(8,128)(2,1)S(1)}, u32[]{:S(2)}) copy-start(bf16[128,256]{0,1:T(8,128)(2,1)S(1)} %copy.96) | copy-start | bytes 196612
  1311.4 778.1 %reduce-scatter.17.cloned.1.call-start = ((), (), s32[]{:S(2)}) async-start(), calls=%async_computation.15 | async-start | bytes 33841152 | tf_op jit(solution)/shard_map/reduce_scatter | solution.py:204
  1325.6 1686.7 %reduce-scatter.15.cloned.1.call-start = ((), (), s32[]{:S(2)}) async-start(), calls=%async_computation.14 | async-start | bytes 67682304 | tf_op jit(solution)/shard_map/reduce_scatter | solution.py:203
  1352.4 1757.7 %all-reduce.14.cloned.1.call-start = ((), (), s32[]{:S(2)}) async-start(), calls=%async_computation.16 | async-start | bytes 6709248 | tf_op jit(solution)/shard_map/psum | solution.py:267
  2092.1 924.5 %copy-start.7 = (bf16[1536,1152]{1,0:T(8,128)(2,1)S(1)}, bf16[1536,1152]{1,0:T(8,128)(2,1)}, u32[]{:S(2)}) copy-start(bf16[1536,1152]{1,0:T(8,128)(2,1)} %all-gather.5.cloned.1.call-done) | copy-start | bytes 10616836
  3015.9 7.9 copy-start.56
  3016.6 5.9 copy-start.58
  3016.6 8.5 copy-start.73
  3016.6 9.8 copy-start.72
  3110.1 11.6 copy-start.17
  3110.1 11.6 copy-start.29
  3110.1 11.6 copy-start.30
  3110.1 12.5 copy-start.35
  3122.6 5.0 copy-start.32
  3122.6 5.0 copy-start.42
  (37 other events, 95.1 us)
Sparse Core Ops, SparseCore 0:
  11.4 135.8 all-gather.4
  150.6 460.2 all-gather.6
  614.3 339.8 all-gather.8
  957.4 181.8 all-gather.10
  1177.7 61.6 reduce-scatter.6
  1243.7 62.4 reduce-scatter.8
  1311.4 136.4 reduce-scatter.12
  1454.1 150.0 reduce-scatter.10
  1611.3 478.1 reduce-scatter.16
  2096.4 915.8 reduce-scatter.14
  3016.6 23.4 all-reduce.13
